TPU v7x, 32 devices: a whole 2x2x4 slice. The times are simulated.
32 devices in a mesh: req: 8 (over z, y), exp: 4 (over x, core).
Axes of the slice: x: 2, y: 2, z: 4, core: 2. Of those that a mesh axis runs over, the one named last changes fastest.
Arguments:
- residual: bfloat16 [4096, 2048], P(('req', 'exp')), may hold values from -3 to 3
- query_vectors: bfloat16 [4096, 2048], P(('req', 'exp')), may hold values from -12 to 12
- key_vectors: bfloat16 [4096, 2048], P(('req', 'exp')), may hold values from -12 to 12
- value_vectors: bfloat16 [4096, 2048], P(('req', 'exp')), may hold values from -6 to 6
- segment_ids: int32 [4096], P('req'), may hold values from 0 to 2, as said below
- prompt_lengths: int32 [8, 3], replicated, may hold values from 1 to 256, as said below
- request_groups: int32 [8], replicated, may hold values from 0 to 7, as said below
- page_table: int32 [8, 4], replicated, may hold values from 0 to 31, as said below
- expert_ids: int32 [4096, 8], P(('req', 'exp')), may hold values from 0 to 15, all different within a row; in each aligned block of 128 rows (0 to 127, 128 to 255, ...) at most 96 rows name the same one
- gate_weights: float32 [4096, 8], P(('req', 'exp')), may hold values from 0.1 to 0.6
- out_weight: bfloat16 [2048, 2048], replicated, may hold values from -0.125 to 0.125
- norm_gain: float32 [2048], replicated, may hold values from 0.5 to 2
- expert_inner: bfloat16 [32, 2048, 1024], P(('req', 'exp')), may hold values from -0.125 to 0.125
- expert_outer: bfloat16 [32, 512, 2048], P(('req', 'exp')), may hold values from -0.1875 to 0.1875
Outputs:
- layer_out: bfloat16 [4096, 2048], P(('req', 'exp'))
- kv_pages: bfloat16 [32, 2, 128, 2048], P('req', None, None, 'exp')
Inputs may be any that keep to these rules, and one draw needn't show every extreme that they name: `prompt_lengths`: each row sums to 512, and its largest entry is 256. `segment_ids`: within each group of 512 rows the numbers never fall; prompt j of the request r with request_groups[r] = g fills prompt_lengths[r, j] consecutive rows of group g. `request_groups`: each group appears once. `page_table`: all entries differ; the 4 pages of one request lie in 4 different owner groups, the owner of slot s being s // 4. `expert_ids`: the 8 ids of a token differ; among the 128 tokens of one device no expert is named more than 96 times, a bound that some block reaches.
All inputs are finite; a program needn't handle non-finite values.
Results may differ from a plain program's by a relative error of at most 0.013.
Values may be sent and summed in bfloat16 or wider, within the bound.
A program may use at most 192 MiB of HBM per device.

v0:
```python
import jax
import jax.numpy as jnp
from jax import lax
from jax.sharding import PartitionSpec as P

HEAD = 128
PAGE = 128


rope_base = 10000.0
norm_eps = 1e-06
masked_score = -1e30


def partner(value, axis, distance):
    return lax.ppermute(value, axis, [(i, i ^ 1 << distance) for i in range(lax.axis_size(axis))])


def rotate(values_in, positions):
    row_count = values_in.shape[0]
    half_head = HEAD // 2
    inverse = rope_base ** (-(2.0 * jnp.arange(half_head, dtype=jnp.float32)) / HEAD)
    angles = positions[:, None] * inverse[None, :]
    cosine = jnp.cos(angles)[:, None, :]
    sines = jnp.sin(angles)[:, None, :]
    shaped = values_in.astype(jnp.float32).reshape(row_count, -1, HEAD)
    first_half = shaped[..., :half_head]
    second_half = shaped[..., half_head:]
    turned = jnp.concatenate(
        [first_half * cosine - second_half * sines, second_half * cosine + first_half * sines],
        axis=-1,
    )
    return turned.reshape(row_count, -1).astype(jnp.bfloat16)


def score_block(query_block, query_segments, key_block, key_segments):
    scores = jnp.einsum(
        "qhd,khd->hqk", query_block, key_block, preferred_element_type=jnp.float32
    ) * HEAD ** (-0.5)
    same_prompt = (query_segments[:, None] == key_segments[None, :])[None]
    return (jnp.where(same_prompt, scores, masked_score), same_prompt)


def attend_all(query_heads, key_heads, value_heads, group_segments, block_rows):
    block_count = query_heads.shape[0] // block_rows

    def one_block(block_index):
        start_row = block_index * block_rows
        query_block = lax.dynamic_slice_in_dim(query_heads, start_row, block_rows, 0)
        query_segments = lax.dynamic_slice_in_dim(group_segments, start_row, block_rows, 0)
        scores, same_prompt = score_block(query_block, query_segments, key_heads, group_segments)
        top_score = jnp.max(scores, axis=-1, keepdims=True)
        weights = jnp.where(same_prompt, jnp.exp(scores - top_score), 0.0)
        totals = jnp.sum(weights, axis=-1)
        mixed = jnp.einsum(
            "hqk,khd->qhd",
            weights.astype(jnp.bfloat16),
            value_heads,
            preferred_element_type=jnp.float32,
        )
        return (mixed / totals.T[:, :, None]).astype(jnp.bfloat16)

    results = lax.map(one_block, jnp.arange(block_count))
    return results.reshape(query_heads.shape[0], -1)


def send_rows(blocks):
    arrived = lax.all_to_all(blocks, ("req", "exp"), split_axis=0, concat_axis=0, tiled=True)
    return arrived


def send_back(blocks):
    arrived = lax.all_to_all(blocks, ("req", "exp"), split_axis=0, concat_axis=0, tiled=True)
    return arrived


def half_expert(rows, inner_half, outer_half):
    projected = jnp.dot(rows, inner_half, preferred_element_type=jnp.float32)
    half_units = projected.shape[1] // 2
    active = (jax.nn.silu(projected[:, :half_units]) * projected[:, half_units:]).astype(
        jnp.bfloat16
    )
    return jnp.dot(active, outer_half, preferred_element_type=jnp.float32)


def on_device(
    residual,
    query_vectors,
    key_vectors,
    value_vectors,
    segment_ids,
    prompt_lengths,
    request_groups,
    page_table,
    expert_ids,
    gate_weights,
    out_weight,
    norm_gain,
    expert_inner,
    expert_outer,
):
    tok_rows, model_width = residual.shape
    req_count = lax.axis_size("req")
    member_count = lax.axis_size("exp")
    device_count = req_count * member_count
    expert_count = device_count // 2
    group_rows = tok_rows * member_count
    top_count = expert_ids.shape[1]
    capacity = 3 * tok_rows * top_count // (2 * expert_count)
    half_capacity = capacity // 2
    page_count = group_rows // PAGE
    group = lax.axis_index("req")
    member = lax.axis_index("exp")
    parity = member % 2
    holds_request = (request_groups == group).astype(jnp.int32)
    my_lengths = jnp.sum(holds_request[:, None] * prompt_lengths, axis=0)
    my_pages = jnp.sum(holds_request[:, None] * page_table, axis=0)
    starts = jnp.cumsum(my_lengths) - my_lengths
    first_row = member * tok_rows
    my_segments = lax.dynamic_slice_in_dim(segment_ids, first_row, tok_rows, 0)
    prompt_index = jnp.arange(prompt_lengths.shape[1], dtype=jnp.int32)
    token_start = jnp.sum(
        jnp.where(my_segments[:, None] == prompt_index[None, :], starts[None, :], 0), axis=1
    )
    positions = (first_row + jnp.arange(tok_rows, dtype=jnp.int32) - token_start).astype(
        jnp.float32
    )
    query_turned = rotate(query_vectors, positions)
    key_turned = rotate(key_vectors, positions)
    query_group, key_group, value_group = (
        lax.all_to_all(query_turned, "exp", split_axis=1, concat_axis=0, tiled=True),
        lax.all_to_all(key_turned, "exp", split_axis=1, concat_axis=0, tiled=True),
        lax.all_to_all(value_vectors, "exp", split_axis=1, concat_axis=0, tiled=True),
    )
    column_count = key_group.shape[1]
    stacked = jnp.stack(
        [
            key_group.reshape(page_count, PAGE, column_count),
            value_group.reshape(page_count, PAGE, column_count),
        ],
        axis=1,
    ).reshape(page_count, -1)
    owner_of_page = my_pages // page_count
    group_range = jnp.arange(req_count, dtype=jnp.int32)
    send_select = (owner_of_page[None, :] == group_range[:, None]).astype(jnp.bfloat16)
    outgoing_pages = jnp.dot(send_select, stacked, preferred_element_type=jnp.float32).astype(
        jnp.bfloat16
    )
    incoming_pages = lax.all_to_all(outgoing_pages, "req", split_axis=0, concat_axis=0, tiled=True)
    source_holds = (request_groups[None, :] == group_range[:, None]).astype(jnp.int32)
    source_pages = jnp.sum(source_holds[:, :, None] * page_table[None, :, :], axis=1)
    slot_ids = group * page_count + jnp.arange(page_count, dtype=jnp.int32)
    place_select = jnp.sum(
        (source_pages[None, :, :] == slot_ids[:, None, None]).astype(jnp.int32), axis=2
    ).astype(jnp.bfloat16)
    kv_pages = (
        jnp.dot(place_select, incoming_pages, preferred_element_type=jnp.float32)
        .astype(jnp.bfloat16)
        .reshape(page_count, 2, PAGE, column_count)
    )
    heads_here = column_count // HEAD
    query_heads = query_group.reshape(group_rows, heads_here, HEAD)
    key_heads = key_group.reshape(group_rows, heads_here, HEAD)
    value_heads = value_group.reshape(group_rows, heads_here, HEAD)
    block_rows = min(512, group_rows)
    attended = attend_all(query_heads, key_heads, value_heads, segment_ids, block_rows)
    token_heads = lax.all_to_all(attended, "exp", split_axis=0, concat_axis=1, tiled=True)
    hidden = residual.astype(jnp.float32) + jnp.dot(
        token_heads, out_weight, preferred_element_type=jnp.float32
    )
    normed = (
        hidden * lax.rsqrt(jnp.mean(hidden * hidden, axis=-1, keepdims=True) + norm_eps) * norm_gain
    ).astype(jnp.bfloat16)
    expert_range = jnp.arange(expert_count, dtype=jnp.int32)
    chosen = (expert_ids[:, :, None] == expert_range[None, None, :]).astype(jnp.int32)
    picked = jnp.sum(chosen, axis=1)
    earlier = jnp.cumsum(picked, axis=0) - picked
    slot_rank = jnp.sum(chosen * earlier[:, None, :], axis=2)
    slot_index = expert_ids * capacity + slot_rank
    slot_range = jnp.arange(expert_count * capacity, dtype=jnp.int32)
    dispatch_matrix = jnp.sum(
        (slot_index[None, :, :] == slot_range[:, None, None]).astype(jnp.int32), axis=2
    ).astype(jnp.bfloat16)
    packed = (
        jnp.dot(dispatch_matrix, normed, preferred_element_type=jnp.float32)
        .astype(jnp.bfloat16)
        .reshape(expert_count, capacity, model_width)
    )
    doubled = jnp.broadcast_to(packed[:, None], (expert_count, 2, capacity, model_width)).reshape(
        device_count, capacity, model_width
    )
    expert_input = send_rows(doubled)
    flat_input = expert_input.reshape(device_count * capacity, model_width)
    partial_out = half_expert(flat_input, expert_inner[0], expert_outer[0]).reshape(
        device_count, capacity, model_width
    )
    kept = lax.dynamic_slice_in_dim(partial_out, parity * half_capacity, half_capacity, 1)
    handed = lax.dynamic_slice_in_dim(partial_out, (1 - parity) * half_capacity, half_capacity, 1)
    received = partner(handed.astype(jnp.bfloat16), "exp", 0).astype(handed.dtype)
    expert_out = (kept + received).astype(jnp.bfloat16)
    returned = send_back(expert_out).reshape(expert_count * capacity, model_width)
    gathered = returned[slot_index]
    mixed = jnp.einsum("tk,tkd->td", gate_weights, gathered.astype(jnp.float32))
    layer_out = (hidden + mixed).astype(jnp.bfloat16)
    return (layer_out, kv_pages)


def solution(mesh):
    placed = (
        P(("req", "exp"), None),
        P(("req", "exp"), None),
        P(("req", "exp"), None),
        P(("req", "exp"), None),
        P("req"),
        P(),
        P(),
        P(),
        P(("req", "exp"), None),
        P(("req", "exp"), None),
        P(),
        P(),
        P(("req", "exp"), None, None),
        P(("req", "exp"), None, None),
    )
    return jax.shard_map(
        on_device,
        mesh=mesh,
        in_specs=placed,
        out_specs=(P(("req", "exp"), None), P("req", None, None, "exp")),
        check_vma=False,
    )
```

profile of v0, /device:TPU:0, one launch (start us, length us, event | category | flops | bytes accessed | tf_op | source)
XLA Modules:
  0.0 634.5 jit_solution(6318942450135649222)
XLA Ops:
  0.7 0.8 compare_convert_fusion
  1.5 0.8 multiply_reduce_fusion.3
  2.3 0.2 reduce-window.8
  2.5 0.8 dynamic_slice.16
  3.3 1.2 copy.84
  4.6 2.2 copy.86
  6.8 0.2 multiply_cosine_fusion
  7.0 2.2 subtract_convert_fusion.1
  9.2 0.8 pad_maximum_fusion.2
  10.0 4.2 all-to-all-start.1
  14.2 1.8 pad_maximum_fusion.1
  16.0 7.1 %all-to-all-done.1 = bf16[128,4,512]{0,2,1:T(8,128)(2,1)S(1)} async-done(((bf16[128,4,512]{0,2,1:T(8,128)(2,1)}), bf16[128,4,512]{0,2,1:T(8,128)(2,1)S(1)}, u32[]{:S(2)}, u32[]{:S(2)}) %all-to-all-start.1) | async-done | bytes 524320 | tf_op jit(solution)/shard_map/all_to_all | solution.py:132
  23.1 3.5 all-to-all-start
  26.5 2.1 copy.90
  28.6 6.8 %all-to-all-done = bf16[128,4,512]{0,2,1:T(8,128)(2,1)S(1)} async-done(((bf16[128,4,512]{0,2,1:T(8,128)(2,1)}), bf16[128,4,512]{0,2,1:T(8,128)(2,1)S(1)}, u32[]{:S(2)}, u32[]{:S(2)}) %all-to-all-start) | async-done | bytes 524320 | tf_op jit(solution)/shard_map/all_to_all | solution.py:131
  35.3 0.8 copy-done.7
  36.1 3.5 all-to-all-start.2
  39.7 0.2 reduce_window_sum.18
  40.0 0.2 broadcast_compare_fusion
  40.3 1.0 copy.87
  41.3 2.0 reshape.262
  43.2 2.0 copy.85
  45.3 2.0 reshape.259
  47.2 1.2 all-to-all-done.2
  48.4 1.0 copy.91
  49.4 2.0 reshape.263
  51.4 1.9 fusion.28
  53.3 2.4 fusion.39
  55.7 1.0 fusion.23
  56.7 0.4 copy.94
  57.1 1.0 all_to_all.67
  58.1 4.0 all-to-all-start.3
  62.1 8.9 %convert_reduce_fusion = s32[1536,128]{1,0:T(8,128)} fusion(s32[128,8]{0,1:T(8,128)S(1)} %get-tuple-element.15), kind=kLoop, calls=%fused_computation.10 | loop fusion | flops 4521984 | bytes 790528 | tf_op jit(solution)/shard_map/reduce_sum | solution.py:181
  71.0 1.0 copy.95
  72.0 5.0 multiply_reduce_fusion
  77.1 1.9 convolution_convert_fusion.2
  78.9 5.6 broadcast_in_dim.60
  84.6 7.3 %all-to-all-start.4 = ((bf16[32,96,2048]{2,1,0:T(8,128)(2,1)}), bf16[32,96,2048]{2,1,0:T(8,128)(2,1)}, u32[]{:S(2)}, u32[]{:S(2)}) async-start(bf16[32,96,2048]{2,1,0:T(8,128)(2,1)} %bitcast.62), calls=%async_computation.4 | async-start | bytes 25165824 | tf_op jit(solution)/shard_map/all_to_all | solution.py:68
  91.9 278.6 %all-to-all-done.4 = bf16[32,96,2048]{2,1,0:T(8,128)(2,1)} async-done(((bf16[32,96,2048]{2,1,0:T(8,128)(2,1)}), bf16[32,96,2048]{2,1,0:T(8,128)(2,1)}, u32[]{:S(2)}, u32[]{:S(2)}) %all-to-all-start.4) | async-done | bytes 12582944 | tf_op jit(solution)/shard_map/all_to_all | solution.py:68
  370.5 17.0 %fusion.5 = f32[3072,1024]{1,0:T(8,128)S(1)} fusion(bf16[3072,2048]{1,0:T(8,128)(2,1)} %bitcast.16, bf16[1,2048,1024]{2,1,0:T(8,128)(2,1)} %param.26), kind=kOutput, calls=%fused_computation.14 | convolution fusion | flops 12884901888 | bytes 29360128 | tf_op jit(solution)/shard_map/dot_general | solution.py:78
  387.5 2.2 fusion.2
  389.8 11.8 %fusion.10 = f32[32,96,2048]{2,1,0:T(8,128)} fusion(bf16[32,96,512]{2,1,0:T(8,128)(2,1)S(1)} %bitcast.74, bf16[1,512,2048]{2,1,0:T(8,128)(2,1)S(1)} %copy-done), kind=kOutput, calls=%fused_computation.22 | convolution fusion | flops 6442450944 | bytes 30408704 | tf_op jit(solution)/shard_map/dot_general | solution.py:83
  401.5 8.4 %dynamic-slice_convert_fusion = bf16[32,48,2048]{2,1,0:T(8,128)(2,1)} fusion(f32[32,96,2048]{2,1,0:T(8,128)} %fusion.10, s32[]{:T(128)S(6)} %select_n.50), kind=kLoop, calls=%fused_computation.6 | loop fusion | bytes 12582916 | tf_op jit(solution)/shard_map/convert_element_type | solution.py:199
  409.9 0.1 multiply_reduce_fusion.2
  410.2 0.7 copy.100
  410.9 0.8 copy.106
  411.7 0.7 fusion.1
  412.4 0.5 broadcast.181
  412.9 2.9 reduce
  415.8 4.7 reshape.286
  420.6 3.6 all-to-all-start.6
  424.2 11.8 %add_convert_fusion = bf16[32,48,2048]{2,1,0:T(8,128)(2,1)} fusion(bf16[32,48,2048]{2,1,0:T(8,128)(2,1)} %collective-permute-done, f32[32,96,2048]{2,1,0:T(8,128)} %fusion.10, s32[]{:T(128)S(6)} %select_n.49), kind=kLoop, calls=%fused_computation.5 | loop fusion | flops 9437184 | bytes 25165828 | tf_op jit(solution)/shard_map/convert_element_type | solution.py:200
  436.0 37.3 %all-to-all-done.6 = bf16[8,2,65536]{2,1,0:T(2,128)(2,1)S(1)} async-done(((bf16[8,2,65536]{2,1,0:T(2,128)(2,1)}), bf16[8,2,65536]{2,1,0:T(2,128)(2,1)S(1)}, u32[]{:S(2)}, u32[]{:S(2)}) %all-to-all-start.6) | async-done | bytes 2097184 | tf_op jit(solution)/shard_map/all_to_all | solution.py:149
  473.3 3.9 all-to-all-start.5
  477.1 0.1 copy.99
  477.3 0.1 copy.103
  477.5 0.1 multiply_reduce_fusion.1
  477.8 4.5 reshape.287
  482.2 4.7 convolution_convert_fusion.1
  486.9 1.2 copy.107
  488.1 129.0 %all-to-all-done.5 = bf16[32,48,2048]{2,1,0:T(8,128)(2,1)} async-done(((bf16[32,48,2048]{2,1,0:T(8,128)(2,1)}), bf16[32,48,2048]{2,1,0:T(8,128)(2,1)}, u32[]{:S(2)}, u32[]{:S(2)}) %all-to-all-start.5) | async-done | bytes 6291488 | tf_op jit(solution)/shard_map/all_to_all | solution.py:73
  617.1 12.6 %gather_fusion = bf16[1024,2048]{1,0:T(8,128)(2,1)} fusion(bf16[1536,2048]{1,0:T(8,128)(2,1)} %bitcast.21, s32[1024]{0:T(1024)S(1)} %broadcast_clamp_fusion), kind=kCustom, calls=%fused_computation | custom fusion | bytes 8392704 | tf_op jit(solution)/shard_map/gather | solution.py:202
  629.6 3.4 fusion.3
  633.0 1.2 fusion.26
  (50 shorter events, 0.7 us)
Async XLA Ops:
  0.6 389.1 %copy-start = (bf16[1,512,2048]{2,1,0:T(8,128)(2,1)S(1)}, bf16[1,512,2048]{2,1,0:T(8,128)(2,1)}, u32[]{:S(2)}) copy-start(bf16[1,512,2048]{2,1,0:T(8,128)(2,1)} %param.27) | copy-start | bytes 6291460
  7.0 32.6 %copy-start.9 = (s32[128,8]{0,1:T(8,128)S(1)}, s32[128,8]{0,1:T(8,128)}, u32[]{:S(2)}) copy-start(s32[128,8]{0,1:T(8,128)} %param.22) | copy-start | bytes 12292
  9.2 30.9 %copy-start.10 = (s32[512]{0:T(512)S(1)}, s32[512]{0:T(512)}, u32[]{:S(2)}) copy-start(s32[512]{0:T(512)} %param.18) | copy-start | bytes 6148
  10.0 13.1 %all-to-all-start.1 = ((bf16[128,4,512]{0,2,1:T(8,128)(2,1)}), bf16[128,4,512]{0,2,1:T(8,128)(2,1)S(1)}, u32[]{:S(2)}, u32[]{:S(2)}) async-start(bf16[128,4,512]{0,2,1:T(8,128)(2,1)} %bitcast.6), calls=%async_computation.1 | async-start | bytes 1048576 | tf_op jit(solution)/shard_map/all_to_all | solution.py:132
  23.1 26.4 %copy-start.3 = (bf16[128,4,512]{0,2,1:T(8,128)(2,1)}, bf16[128,4,512]{0,2,1:T(8,128)(2,1)S(1)}, u32[]{:S(2)}) copy-start(bf16[128,4,512]{0,2,1:T(8,128)(2,1)S(1)} %all-to-all-done.1) | copy-start | bytes 1572868
  23.1 12.3 %all-to-all-start = ((bf16[128,4,512]{0,2,1:T(8,128)(2,1)}), bf16[128,4,512]{0,2,1:T(8,128)(2,1)S(1)}, u32[]{:S(2)}, u32[]{:S(2)}) async-start(bf16[128,4,512]{0,2,1:T(8,128)(2,1)} %bitcast.78), calls=%async_computation | async-start | bytes 1048576 | tf_op jit(solution)/shard_map/all_to_all | solution.py:131
  35.3 0.8 copy-start.7
  36.1 12.3 %all-to-all-start.2 = ((bf16[128,4,512]{0,2,1:T(8,128)(2,1)}), bf16[128,4,512]{0,2,1:T(8,128)(2,1)S(1)}, u32[]{:S(2)}, u32[]{:S(2)}) async-start(bf16[128,4,512]{0,2,1:T(8,128)(2,1)} %bitcast.76), calls=%async_computation.2 | async-start | bytes 1048576 | tf_op jit(solution)/shard_map/all_to_all | solution.py:133
  48.4 7.3 %copy-start.5 = (bf16[128,4,512]{0,2,1:T(8,128)(2,1)}, bf16[128,4,512]{0,2,1:T(8,128)(2,1)S(1)}, u32[]{:S(2)}) copy-start(bf16[128,4,512]{0,2,1:T(8,128)(2,1)S(1)} %all-to-all-done.2) | copy-start | bytes 1572868
  53.3 2.4 copy-start.8
  58.1 12.9 %all-to-all-start.3 = ((bf16[4,128,512]{2,1,0:T(8,128)(2,1)}), bf16[4,128,512]{2,1,0:T(8,128)(2,1)S(1)}, u32[]{:S(2)}, u32[]{:S(2)}) async-start(bf16[4,128,512]{2,1,0:T(8,128)(2,1)} %all_to_all.67), calls=%async_computation.3 | async-start | bytes 1048576 | tf_op jit(solution)/shard_map/all_to_all | solution.py:167
  72.0 5.0 copy-start.2
  72.0 5.0 copy-start.12
  84.6 286.0 %all-to-all-start.4 = ((bf16[32,96,2048]{2,1,0:T(8,128)(2,1)}), bf16[32,96,2048]{2,1,0:T(8,128)(2,1)}, u32[]{:S(2)}, u32[]{:S(2)}) async-start(bf16[32,96,2048]{2,1,0:T(8,128)(2,1)} %bitcast.62), calls=%async_computation.4 | async-start | bytes 25165824 | tf_op jit(solution)/shard_map/all_to_all | solution.py:68
  401.5 8.4 %copy-start.11 = (s32[8,4]{0,1:T(4,128)S(1)}, s32[8,4]{0,1:T(4,128)}, u32[]{:S(2)}) copy-start(s32[8,4]{0,1:T(4,128)} %param.21) | copy-start | bytes 388
  401.5 8.5 %copy-start.4 = (bf16[128,4,512]{0,2,1:T(8,128)(2,1)S(1)}, bf16[128,4,512]{0,2,1:T(8,128)(2,1)}, u32[]{:S(2)}) copy-start(bf16[128,4,512]{0,2,1:T(8,128)(2,1)} %copy-done.3) | copy-start | bytes 1572868
  401.5 8.5 %copy-start.6 = (bf16[128,4,512]{0,2,1:T(8,128)(2,1)S(1)}, bf16[128,4,512]{0,2,1:T(8,128)(2,1)}, u32[]{:S(2)}) copy-start(bf16[128,4,512]{0,2,1:T(8,128)(2,1)} %copy-done.5) | copy-start | bytes 1572868
  409.9 14.3 %collective-permute-start = (bf16[32,48,2048]{2,1,0:T(8,128)(2,1)}, bf16[32,48,2048]{2,1,0:T(8,128)(2,1)}, u32[]{:S(2)}, u32[]{:S(2)}) collective-permute-start(bf16[32,48,2048]{2,1,0:T(8,128)(2,1)} %dynamic-slice_convert_fusion), channel_id=1, source_target_pairs={{0,1},{1,0},{2,3},{3,2},{4,5},{5,4},{6,7},{7,6},{8,9},{9,8},{10,11... | collective-permute-start | bytes 18874376 | tf_op jit(solution)/shard_map/ppermute | solution.py:16
  420.6 52.7 %all-to-all-start.6 = ((bf16[8,2,65536]{2,1,0:T(2,128)(2,1)}), bf16[8,2,65536]{2,1,0:T(2,128)(2,1)S(1)}, u32[]{:S(2)}, u32[]{:S(2)}) async-start(bf16[8,2,65536]{2,1,0:T(2,128)(2,1)} %reshape.286), calls=%async_computation.6 | async-start | bytes 4194304 | tf_op jit(solution)/shard_map/all_to_all | solution.py:149
  436.0 41.4 %copy-start.13 = (f32[128,8]{0,1:T(8,128)S(1)}, f32[128,8]{0,1:T(8,128)}, u32[]{:S(2)}) copy-start(f32[128,8]{0,1:T(8,128)} %param.23) | copy-start | bytes 12292
  436.0 41.5 %copy-start.14 = (s32[8]{0:T(128)S(1)}, s32[8]{0:T(128)}, u32[]{:S(2)}) copy-start(s32[8]{0:T(128)} %param.20) | copy-start | bytes 100
  473.3 143.8 %all-to-all-start.5 = ((bf16[32,48,2048]{2,1,0:T(8,128)(2,1)}), bf16[32,48,2048]{2,1,0:T(8,128)(2,1)}, u32[]{:S(2)}, u32[]{:S(2)}) async-start(bf16[32,48,2048]{2,1,0:T(8,128)(2,1)} %add_convert_fusion), calls=%async_computation.5 | async-start | bytes 12582912 | tf_op jit(solution)/shard_map/all_to_all | solution.py:73
  617.1 17.2 %copy-start.1 = (bf16[1,512,2048]{2,1,0:T(8,128)(2,1)S(1)}, bf16[1,512,2048]{2,1,0:T(8,128)(2,1)}, u32[]{:S(2)}) copy-start(bf16[1,512,2048]{2,1,0:T(8,128)(2,1)} %param.27) | copy-start | bytes 6291460
where the time goes:
time: 641 us; the launch traced here: 634 us
  waiting for transfers between devices  460 us (72%)
  local copies, waits for them, and re-layouts  58.9 us (9%)
  matrix products  47.2 us (7%)
  other arithmetic  37.2 us (6%)
  starting transfers between devices  29.9 us (5%)
    all_to_all x1, waiting for transfers between devices, send_rows(): lax.all_to_all(blocks, ('req', 'exp'), split_axis=0, concat_axis=0, tiled...  279 us
    all_to_all x1, waiting for transfers between devices, send_back(): lax.all_to_all(blocks, ('req', 'exp'), split_axis=0, concat_axis=0, tiled...  129 us
    all_to_all x1, waiting for transfers between devices, on_device(): lax.all_to_all(outgoing_pages, 'req', split_axis=0, concat_axis=0, tiled=...  37.3 us
    dot_general x1, matrix products, half_expert(): projected = jnp.dot(rows, inner_half, preferred_element_type=jnp.float32)  17 us
    unnamed x36, local copies, waits for them, and re-layouts  14.2 us
  transfers between devices with their start and end apart: 8, of which 6 were waited for; matrix products, arithmetic and copies ran while one was open for 8% of the time, Pallas kernels for 0%

commit v1 on v0

v1 whole, which is shorter than its diff:
```python
import functools

import jax
import jax.numpy as jnp
from jax import lax
from jax.experimental import pallas as pl
from jax.experimental.pallas import tpu as pltpu
from jax.sharding import PartitionSpec as P

HEAD = 128
PAGE = 128

rope_base = 10000.0
norm_eps = 1e-06
masked_score = -1e30
CHUNKS = 2


def turn(block, cosine, sines):
    wide = block.astype(jnp.float32)
    return (wide * cosine + pltpu.roll(wide, HEAD // 2, 1) * sines).astype(jnp.bfloat16)


def turn_keys_kernel(key_ref, value_ref, cos_ref, sin_ref, out_ref):
    width = key_ref.shape[1]
    cosine, sines = cos_ref[...], sin_ref[...]
    for start in range(0, width, HEAD):
        out_ref[:, start : start + HEAD] = turn(
            key_ref[:, start : start + HEAD], cosine, sines
        )
    out_ref[:, width:] = value_ref[...]


def turn_keys(keys, values, cosine, sines):
    rows, width = keys.shape
    return pl.pallas_call(
        turn_keys_kernel,
        out_shape=jax.ShapeDtypeStruct((rows, 2 * width), jnp.bfloat16),
        compiler_params=pltpu.CompilerParams(vmem_limit_bytes=32 << 20),
        name="turn_keys",
    )(keys, values, cosine, sines)


def attention_kernel(query_ref, key_ref, value_ref, cos_ref, sin_ref, mine_ref, all_ref, out_ref):
    cosine, sines = cos_ref[...], sin_ref[...]
    same = mine_ref[...] == all_ref[...]
    for start in range(0, query_ref.shape[1], HEAD):
        cols = slice(start, start + HEAD)
        query = turn(query_ref[:, cols], cosine, sines)
        scores = lax.dot_general(
            query, key_ref[:, cols], (((1,), (1,)), ((), ())), preferred_element_type=jnp.float32
        ) * HEAD ** (-0.5)
        scores = jnp.where(same, scores, masked_score)
        weights = jnp.where(same, jnp.exp(scores - jnp.max(scores, axis=1, keepdims=True)), 0.0)
        totals = jnp.sum(weights, axis=1, keepdims=True)
        mixed = jnp.dot(
            weights.astype(jnp.bfloat16), value_ref[:, cols], preferred_element_type=jnp.float32
        )
        out_ref[:, cols] = (mixed / totals).astype(jnp.bfloat16)


def attend(queries, keys_values, cosine, sines, my_segments, segments):
    rows, width = queries.shape
    all_rows = keys_values.shape[0]
    step = 512
    steps = width // step
    return pl.pallas_call(
        attention_kernel,
        grid=(steps,),
        in_specs=[
            pl.BlockSpec((rows, step), lambda i: (0, i)),
            pl.BlockSpec((all_rows, step), lambda i: (0, i)),
            pl.BlockSpec((all_rows, step), lambda i: (0, i + steps)),
            pl.BlockSpec((rows, HEAD), lambda i: (0, 0)),
            pl.BlockSpec((rows, HEAD), lambda i: (0, 0)),
            pl.BlockSpec((rows, 1), lambda i: (0, 0)),
            pl.BlockSpec((1, all_rows), lambda i: (0, 0)),
        ],
        out_specs=pl.BlockSpec((rows, step), lambda i: (0, i)),
        out_shape=jax.ShapeDtypeStruct((rows, width), jnp.bfloat16),
        compiler_params=pltpu.CompilerParams(vmem_limit_bytes=32 << 20),
        name="attend",
    )(queries, keys_values, keys_values, cosine, sines, my_segments[:, None], segments[None, :])


def pack_kernel(index_ref, key_ref, value_ref, out_ref):
    out_ref[0, 0] = key_ref[0]
    out_ref[0, 1] = value_ref[0]


def pack_pages(pages, index, columns, member_count):
    count = index.shape[0] - 1
    return pl.pallas_call(
        pack_kernel,
        grid_spec=pltpu.PrefetchScalarGridSpec(
            num_scalar_prefetch=1,
            grid=(count,),
            in_specs=[
                pl.BlockSpec((1, PAGE, columns), lambda i, index: (index[i], 0, index[count])),
                pl.BlockSpec(
                    (1, PAGE, columns), lambda i, index: (index[i], 0, index[count] + member_count)
                ),
            ],
            out_specs=pl.BlockSpec((1, 2, PAGE, columns), lambda i, index: (i, 0, 0, 0)),
        ),
        out_shape=jax.ShapeDtypeStruct((count, 2, PAGE, columns), jnp.bfloat16),
        name="pack_pages",
    )(index, pages, pages)


def place_kernel(index_ref, in_ref, out_ref):
    out_ref[...] = in_ref[...]


def place_pages(incoming, index):
    block = (1,) + incoming.shape[1:]
    return pl.pallas_call(
        place_kernel,
        grid_spec=pltpu.PrefetchScalarGridSpec(
            num_scalar_prefetch=1,
            grid=index.shape,
            in_specs=[pl.BlockSpec(block, lambda i, index: (index[i], 0, 0, 0))],
            out_specs=pl.BlockSpec(block, lambda i, index: (i, 0, 0, 0)),
        ),
        out_shape=jax.ShapeDtypeStruct(index.shape + incoming.shape[1:], jnp.bfloat16),
        name="place_pages",
    )(index, incoming)


def expert_kernel(rows_ref, gate_ref, inner_ref, outer_ref, out_ref):
    projected = jnp.dot(rows_ref[...], inner_ref[0], preferred_element_type=jnp.float32)
    half = projected.shape[1] // 2
    first = projected[:, :half]
    active = (first / (1.0 + jnp.exp(-first)) * projected[:, half:]).astype(jnp.bfloat16)
    out = jnp.dot(active, outer_ref[0], preferred_element_type=jnp.float32)
    out_ref[...] = (out * gate_ref[...]).astype(jnp.bfloat16)


def half_expert(rows, gates, inner, outer):
    count, width = rows.shape
    step = min(512, count)
    once = pl.Buffered(1)
    return pl.pallas_call(
        expert_kernel,
        grid=(count // step,),
        in_specs=[
            pl.BlockSpec((step, width), lambda i: (i, 0)),
            pl.BlockSpec((step, 1), lambda i: (i, 0)),
            pl.BlockSpec(inner.shape, lambda i: (0, 0, 0), pipeline_mode=once),
            pl.BlockSpec(outer.shape, lambda i: (0, 0, 0), pipeline_mode=once),
        ],
        out_specs=pl.BlockSpec((step, width), lambda i: (i, 0)),
        out_shape=jax.ShapeDtypeStruct((count, width), jnp.bfloat16),
        compiler_params=pltpu.CompilerParams(vmem_limit_bytes=48 << 20),
        cost_estimate=pl.CostEstimate(
            flops=2 * count * width * (inner.shape[2] + outer.shape[1]),
            bytes_accessed=4 * count * width,
            transcendentals=0,
        ),
        name="half_expert",
    )(rows, gates, inner, outer)


def on_device(
    residual,
    query_vectors,
    key_vectors,
    value_vectors,
    segment_ids,
    prompt_lengths,
    request_groups,
    page_table,
    expert_ids,
    gate_weights,
    out_weight,
    norm_gain,
    expert_inner,
    expert_outer,
):
    tok_rows, model_width = residual.shape
    req_count = lax.axis_size("req")
    member_count = lax.axis_size("exp")
    device_count = req_count * member_count
    expert_count = device_count // 2
    group_rows = tok_rows * member_count
    page_count = group_rows // PAGE
    columns = model_width // member_count
    everyone = ("req", "exp")
    group = lax.axis_index("req")
    member = lax.axis_index("exp")
    expert = (group * member_count + member) // 2

    holds_request = (request_groups == group).astype(jnp.int32)
    my_lengths = jnp.sum(holds_request[:, None] * prompt_lengths, axis=0)
    my_pages = jnp.sum(holds_request[:, None] * page_table, axis=0)
    first_row = member * tok_rows
    my_segments = lax.dynamic_slice_in_dim(segment_ids, first_row, tok_rows, 0)
    prompt_index = jnp.arange(prompt_lengths.shape[1], dtype=jnp.int32)
    token_start = jnp.sum(
        jnp.where(prompt_index[None, :] < my_segments[:, None], my_lengths[None, :], 0), axis=1
    )
    positions = (first_row + jnp.arange(tok_rows, dtype=jnp.int32) - token_start).astype(
        jnp.float32
    )
    inverse = rope_base ** (-(2.0 * jnp.arange(HEAD // 2, dtype=jnp.float32)) / HEAD)
    angles = positions[:, None] * inverse[None, :]
    cosine, sines = jnp.cos(angles), jnp.sin(angles)
    cosine = jnp.concatenate([cosine, cosine], axis=1)
    sines = jnp.concatenate([-sines, sines], axis=1)

    mine = turn_keys(key_vectors, value_vectors, cosine, sines)
    keys_values = lax.all_gather(mine, "exp", axis=0, tiled=True)

    expert_range = jnp.arange(expert_count, dtype=jnp.int32)
    dense_gates = jnp.sum(
        jnp.where(
            expert_ids.T[None] == expert_range[:, None, None], gate_weights.T[None], 0.0
        ),
        axis=1,
    )
    all_gates = lax.all_gather(dense_gates, everyone, axis=0)
    my_gates = lax.dynamic_index_in_dim(all_gates, expert, 1, keepdims=False)

    group_range = jnp.arange(req_count, dtype=jnp.int32)
    page_range = jnp.arange(page_count, dtype=jnp.int32)
    owned = my_pages[None, :] // page_count == group_range[:, None]
    page_for_group = jnp.sum(jnp.where(owned, page_range[None, :], 0), axis=1)
    outgoing = pack_pages(
        keys_values.reshape(page_count, PAGE, 2 * model_width),
        jnp.concatenate([page_for_group, member[None]]).astype(jnp.int32),
        columns,
        member_count,
    )
    incoming = lax.all_to_all(outgoing, "req", split_axis=0, concat_axis=0, tiled=True)
    slot_ids = group * page_count + page_range
    holds_slot = jnp.any(page_table[None, :, :] == slot_ids[:, None, None], axis=2)
    source_of_slot = jnp.sum(jnp.where(holds_slot, request_groups[None, :], 0), axis=1)
    kv_pages = place_pages(incoming, source_of_slot.astype(jnp.int32))

    attention = attend(query_vectors, keys_values, cosine, sines, my_segments, segment_ids)
    hidden = residual.astype(jnp.float32) + jnp.dot(
        attention, out_weight, preferred_element_type=jnp.float32
    )
    normed = (
        hidden * lax.rsqrt(jnp.mean(hidden * hidden, axis=-1, keepdims=True) + norm_eps) * norm_gain
    ).astype(jnp.bfloat16)

    part = tok_rows // CHUNKS
    sums = []
    for chunk in range(CHUNKS):
        rows = slice(chunk * part, (chunk + 1) * part)
        gathered = lax.all_gather(normed[rows], everyone, axis=0, tiled=True)
        gates = my_gates[:, rows].reshape(-1, 1)
        partial_out = half_expert(gathered, gates, expert_inner, expert_outer)
        summed = lax.psum_scatter(partial_out, everyone, scatter_dimension=0, tiled=True)
        sums.append(hidden[rows] + summed.astype(jnp.float32))
    layer_out = jnp.concatenate(sums, axis=0).astype(jnp.bfloat16)
    return (layer_out, kv_pages)


def solution(mesh):
    placed = (
        P(("req", "exp"), None),
        P(("req", "exp"), None),
        P(("req", "exp"), None),
        P(("req", "exp"), None),
        P("req"),
        P(),
        P(),
        P(),
        P(("req", "exp"), None),
        P(("req", "exp"), None),
        P(),
        P(),
        P(("req", "exp"), None, None),
        P(("req", "exp"), None, None),
    )
    return jax.shard_map(
        on_device,
        mesh=mesh,
        in_specs=placed,
        out_specs=(P(("req", "exp"), None), P("req", None, None, "exp")),
        check_vma=False,
    )
```

time: 641 us -> 539 us (0.84); the launches traced: 634 us -> 539 us
  waiting for transfers between devices: 460 us -> 405 us
  Pallas kernels: 0 us -> 53.2 us
  matrix products: 47.2 us -> 1.4 us
  local copies, waits for them, and re-layouts: 58.9 us -> 13.7 us
  blocking collectives: 0 us -> 41.9 us
  other arithmetic: 37.2 us -> 5.65 us
  starting transfers between devices: 29.9 us -> 4.38 us
  between operations: 1.29 us -> 14 us
    all_to_all x7 -> x1, waiting for transfers between devices: 460 us -> 57.2 us  [on_device(): lax.all_to_all(outgoing, 'req', split_axis=0, concat_axis=0, tiled=True)]
    reduce_scatter x0 -> x2, waiting for transfers between devices: none -> 216 us  [on_device(): lax.psum_scatter(partial_out, everyone, scatter_dimension=0, tiled=True)]
    all_gather x0 -> x3, waiting for transfers between devices: none -> 131 us  [the longest x2 94.1 us: on_device(): gathered = lax.all_gather(normed[rows], everyone, axis=0, tiled=True)]
    pallas_call x0 -> x6, Pallas kernels: none -> 53.2 us  [the longest x2 36.3 us: half_expert(): pl.pallas_call(expert_kernel, grid=(count // step,), in_specs=[pl.BlockSp...]
    dot_general x9 -> x1, matrix products: 47.2 us -> 1.4 us  [on_device(): jnp.dot(attention, out_weight, preferred_element_type=jnp.float32)]
    all_gather x0 -> x1, blocking collectives: none -> 41.9 us  [on_device(): all_gates = lax.all_gather(dense_gates, everyone, axis=0)]
    all_to_all x7 -> x1, starting transfers between devices: 29.9 us -> 4.18 us  [on_device(): lax.all_to_all(outgoing, 'req', split_axis=0, concat_axis=0, tiled=True)]
    convert_element_type x4 -> x1, other arithmetic: 15.2 us -> 0.15 us  [on_device(): normed = (hidden * lax.rsqrt(jnp.mean(hidden * hidden, axis=-1, keepdims=...]
  transfers between devices with their start and end apart: 8 -> 6, of which waited for: 6 -> 6; matrix products, arithmetic and copies ran while one was open for 8% -> 1% of each run, Pallas kernels for 0% -> 9%
where the time goes in v1:
time: 539 us
  waiting for transfers between devices  405 us (75%)
  Pallas kernels  53.2 us (10%)
  blocking collectives  41.9 us (8%)
  between operations  14 us (3%)
  local copies, waits for them, and re-layouts  13.7 us (3%)
  other arithmetic  5.65 us (1%)
    reduce_scatter x2, waiting for transfers between devices, on_device(): lax.psum_scatter(partial_out, everyone, scatter_dimension=0, tiled=True)  216 us
    all_gather x2, waiting for transfers between devices, on_device(): gathered = lax.all_gather(normed[rows], everyone, axis=0, tiled=True)  94.1 us
    all_to_all x1, waiting for transfers between devices, on_device(): lax.all_to_all(outgoing, 'req', split_axis=0, concat_axis=0, tiled=True)  57.2 us
    all_gather x1, blocking collectives, on_device(): all_gates = lax.all_gather(dense_gates, everyone, axis=0)  41.9 us
    all_gather x1, waiting for transfers between devices, on_device(): keys_values = lax.all_gather(mine, 'exp', axis=0, tiled=True)  36.5 us
    pallas_call x2, Pallas kernels, half_expert(): pl.pallas_call(expert_kernel, grid=(count // step,), in_specs=[pl.BlockSp...  36.3 us
  transfers between devices with their start and end apart: 6, of which 6 were waited for; matrix products, arithmetic and copies ran while one was open for 1% of the time, Pallas kernels for 9%

profile of v1, /device:TPU:0, one launch (start us, length us, event | category | flops | bytes accessed | tf_op | source)
XLA Modules:
  0.0 538.9 jit_solution(4155785227209608579)
XLA Ops:
  7.2 0.0 copy-start.10
  7.2 0.0 all-gather.5.cloned.1.call-start
  7.2 0.8 dynamic_slice.7
  8.1 0.7 compare_convert_fusion
  8.7 0.8 multiply_reduce_fusion.2
  9.5 0.1 select_reduce_fusion.3
  9.6 0.3 fusion.2
  9.9 0.1 pad_maximum_fusion.1
  10.0 0.0 copy-start.1
  10.0 1.0 copy-done.1
  11.1 1.0 copy-done.2
  12.1 1.3 turn_keys.1
  13.4 0.0 all-gather.5.cloned.1.call-update
  13.4 0.0 all-gather.9.cloned.1.call-start
  13.5 0.8 dynamic-slice_bitcast_fusion
  14.2 0.1 copy.22.mine_ref
  14.3 36.5 %all-gather.5.cloned.1.call-done.key_ref.value_ref = bf16[512,4096]{1,0:T(8,128)(2,1)} async-done(((bf16[128,4096]{1,0:T(8,128)(2,1)}), bf16[512,4096]{1,0:T(8,128)(2,1)}) %all-gather.5.cloned.1.call-update) | async-done | bytes 4194320 | tf_op jit(solution)/shard_map/all_gather | solution.py:212
  50.8 2.2 copy-done
  53.0 1.0 copy-done.3
  54.0 0.7 copy-done.4
  54.7 5.5 %attend.1 = bf16[128,2048]{1,0:T(8,128)(2,1)S(1)} custom-call(bf16[128,2048]{1,0:T(8,128)(2,1)S(1)} %copy-done.3, bf16[512,4096]{1,0:T(8,128)(2,1)S(1)} %copy-done, bf16[512,4096]{1,0:T(8,128)(2,1)S(1)} %copy-done, f32[128,128]{1,0:T(8,128)S(1)} %get-tuple-element.13.cos_ref, f32[128,128]{1,0:T(8,128)S(1)} %get-tuple-element.14.sin_ref, ...), custom_call_target="tpu_custom_call" | custom-call | tf_op jit(solution)/shard_map/attend/pallas_call | solution.py:67
  60.2 0.0 copy-done.10
  60.2 0.0 copy-done.6
  60.3 0.0 copy-start.11
  60.3 0.0 copy-start.13
  60.3 0.0 copy-start.14
  60.3 0.0 copy-start.5
  60.3 1.4 multiply_reduce_fusion
  61.7 1.0 copy-done.7
  62.8 0.0 copy-done.11
  62.8 0.2 multiply_convert_fusion
  62.9 0.8 fusion.3
  63.8 0.0 all-gather.9.cloned.1.call-update
  63.8 0.0 all-gather.7.cloned.1.call-start
  63.8 0.7 all-gather.7.cloned.1.call-update
  64.5 0.0 reduce-scatter.5.cloned.1.call-start
  64.6 41.9 %all-gather = f32[512,128]{1,0:T(8,128)S(1)} all-gather(f32[16,128]{1,0:T(8,128)S(1)} %select_reduce_fusion), channel_id=2, replica_groups=mesh['req'=8,'exp'=4] {'req','exp'}, dimensions={0}, use_global_device_ids=true | all-gather | bytes 270336 | tf_op jit(solution)/shard_map/all_gather | solution.py:221
  106.6 0.1 fusion.4
  106.7 1.0 reshape.88.gate_ref
  107.7 33.9 %all-gather.9.cloned.1.call-done.rows_ref = bf16[2048,2048]{1,0:T(8,128)(2,1)} async-done(((bf16[64,2048]{1,0:T(8,128)(2,1)}), bf16[2048,2048]{1,0:T(8,128)(2,1)}) %all-gather.9.cloned.1.call-update) | async-done | bytes 8388624 | tf_op jit(solution)/shard_map/all_gather | solution.py:252
  141.6 0.0 copy-done.5
  141.6 18.2 %half_expert.3 = bf16[2048,2048]{1,0:T(8,128)(2,1)} custom-call(bf16[2048,2048]{1,0:T(8,128)(2,1)} %all-gather.9.cloned.1.call-done.rows_ref, f32[2048,1]{1,0:T(8,128)S(1)} %reshape.88.gate_ref, bf16[1,2048,1024]{2,1,0:T(8,128)(2,1)} %inner_ref.3, bf16[1,512,2048]{2,1,0:T(8,128)(2,1)S(1)} %copy-done.5), custom_call_target="tpu_custom_call" | custom-call | flops 12884901888 | bytes 16777216 | tf_op jit(solution)/shard_map/half_expert/pallas_call | solution.py:143
  159.7 0.0 reduce-scatter.5.cloned.1.call-update
  159.8 0.0 reduce-scatter.3.cloned.1.call-start
  159.8 1.0 reshape.87.gate_ref
  160.8 60.2 %all-gather.7.cloned.1.call-done.rows_ref = bf16[2048,2048]{1,0:T(8,128)(2,1)} async-done(((bf16[64,2048]{1,0:T(8,128)(2,1)}), bf16[2048,2048]{1,0:T(8,128)(2,1)}) %all-gather.7.cloned.1.call-update) | async-done | bytes 8388624 | tf_op jit(solution)/shard_map/all_gather | solution.py:252
  221.0 18.1 %half_expert.2 = bf16[2048,2048]{1,0:T(8,128)(2,1)} custom-call(bf16[2048,2048]{1,0:T(8,128)(2,1)} %all-gather.7.cloned.1.call-done.rows_ref, f32[2048,1]{1,0:T(8,128)S(1)} %reshape.87.gate_ref, bf16[1,2048,1024]{2,1,0:T(8,128)(2,1)} %inner_ref.3, bf16[1,512,2048]{2,1,0:T(8,128)(2,1)S(1)} %copy-done.5), custom_call_target="tpu_custom_call" | custom-call | flops 12884901888 | bytes 16777216 | tf_op jit(solution)/shard_map/half_expert/pallas_call | solution.py:143
  239.1 0.0 reduce-scatter.3.cloned.1.call-update
  239.2 0.7 copy-done.12
  239.8 0.1 multiply_reduce_fusion.1
  239.9 0.1 select_reduce_fusion.1
  240.0 0.6 pad_add_fusion.index_ref
  240.6 6.1 %pack_pages.1 = bf16[8,2,128,512]{3,2,1,0:T(8,128)(2,1)} custom-call(s32[9]{0:T(128)} %pad_add_fusion.index_ref, bf16[4,128,4096]{2,1,0:T(8,128)(2,1)} %bitcast.11, bf16[4,128,4096]{2,1,0:T(8,128)(2,1)} %bitcast.12), custom_call_target="tpu_custom_call" | custom-call | tf_op jit(solution)/shard_map/pack_pages/pallas_call | solution.py:93
  246.8 4.2 all-to-all-start
  250.9 0.1 compare_reduce_fusion
  251.0 0.6 select_reduce_fusion.2.index_ref
  251.7 57.2 %all-to-all-done.in_ref = bf16[8,2,128,512]{3,2,1,0:T(8,128)(2,1)S(1)} async-done(((bf16[8,2,128,512]{3,2,1,0:T(8,128)(2,1)}), bf16[8,2,128,512]{3,2,1,0:T(8,128)(2,1)S(1)}, u32[]{:S(2)}, u32[]{:S(2)}) %all-to-all-start) | async-done | bytes 2097184 | tf_op jit(solution)/shard_map/all_to_all | solution.py:234
  308.9 1.3 copy-done.9
  310.2 4.0 place_pages.1
  314.3 67.2 %reduce-scatter.5.cloned.1.call-done = bf16[64,2048]{1,0:T(8,128)(2,1)} async-done(((bf16[2048,2048]{1,0:T(8,128)(2,1)}), bf16[64,2048]{1,0:T(8,128)(2,1)}) %reduce-scatter.5.cloned.1.call-update) | async-done | bytes 262160 | tf_op jit(solution)/shard_map/reduce_scatter | solution.py:255
  381.5 148.9 %reduce-scatter.3.cloned.1.call-done = bf16[64,2048]{1,0:T(8,128)(2,1)} async-done(((bf16[2048,2048]{1,0:T(8,128)(2,1)}), bf16[64,2048]{1,0:T(8,128)(2,1)}) %reduce-scatter.3.cloned.1.call-update) | async-done | bytes 262160 | tf_op jit(solution)/shard_map/reduce_scatter | solution.py:255
  530.4 0.0 copy-done.8
  530.4 1.1 fusion.1
  531.5 0.8 pad_maximum_fusion
  (20 shorter events, 0.1 us)
Async XLA Ops:
  7.2 53.1 %copy-start.10 = (bf16[128,2048]{1,0:T(8,128)(2,1)S(1)}, bf16[128,2048]{1,0:T(8,128)(2,1)}, u32[]{:S(2)}) copy-start(bf16[128,2048]{1,0:T(8,128)(2,1)} %param.14) | copy-start | bytes 1572868
  7.2 43.6 %all-gather.5.cloned.1.call-start = ((), (), s32[]{:S(2)}) async-start(), calls=%async_computation.3 | async-start | bytes 5242880 | tf_op jit(solution)/shard_map/all_gather | solution.py:212
  10.0 1.0 copy-start.1
  11.1 1.0 copy-start.2
  13.4 128.2 %all-gather.9.cloned.1.call-start = ((), (), s32[]{:S(2)}) async-start(), calls=%async_computation.6 | async-start | bytes 8650752 | tf_op jit(solution)/shard_map/all_gather | solution.py:252
  50.8 2.2 copy-start
  53.0 1.0 copy-start.3
  54.0 0.7 copy-start.4
  54.7 5.5 %copy-start.6 = (bf16[2048,2048]{1,0:T(8,128)(2,1)S(1)}, bf16[2048,2048]{1,0:T(8,128)(2,1)}, u32[]{:S(2)}) copy-start(bf16[2048,2048]{1,0:T(8,128)(2,1)} %param.24) | copy-start | bytes 25165828
  60.3 2.5 copy-start.11
  60.3 4.3 copy-start.13
  60.3 4.3 copy-start.14
  60.3 81.3 %copy-start.5 = (bf16[1,512,2048]{2,1,0:T(8,128)(2,1)S(1)}, bf16[1,512,2048]{2,1,0:T(8,128)(2,1)}, u32[]{:S(2)}) copy-start(bf16[1,512,2048]{2,1,0:T(8,128)(2,1)} %outer_ref.3) | copy-start | bytes 6291460
  61.7 1.1 copy-start.7
  63.8 157.2 %all-gather.7.cloned.1.call-start = ((), (), s32[]{:S(2)}) async-start(), calls=%async_computation.4 | async-start | bytes 8650752 | tf_op jit(solution)/shard_map/all_gather | solution.py:252
  64.5 317.0 %reduce-scatter.5.cloned.1.call-start = ((), (), s32[]{:S(2)}) async-start(), calls=%async_computation.7 | async-start | bytes 8650752 | tf_op jit(solution)/shard_map/reduce_scatter | solution.py:255
  159.8 370.6 %reduce-scatter.3.cloned.1.call-start = ((), (), s32[]{:S(2)}) async-start(), calls=%async_computation.5 | async-start | bytes 8650752 | tf_op jit(solution)/shard_map/reduce_scatter | solution.py:255
  239.1 0.7 copy-start.12
  239.8 11.2 %copy-start.15 = (s32[8]{0:T(128)S(1)}, s32[8]{0:T(128)}, u32[]{:S(2)}) copy-start(s32[8]{0:T(128)} %param.20) | copy-start | bytes 100
  240.6 289.8 %copy-start.8 = (f32[128,2048]{1,0:T(8,128)S(1)}, f32[128,2048]{1,0:T(8,128)}, u32[]{:S(2)}) copy-start(f32[128,2048]{1,0:T(8,128)} %copy-done.7) | copy-start | bytes 3145732
  246.8 62.1 %all-to-all-start = ((bf16[8,2,128,512]{3,2,1,0:T(8,128)(2,1)}), bf16[8,2,128,512]{3,2,1,0:T(8,128)(2,1)S(1)}, u32[]{:S(2)}, u32[]{:S(2)}) async-start(bf16[8,2,128,512]{3,2,1,0:T(8,128)(2,1)} %pack_pages.1), calls=%async_computation.2 | async-start | bytes 4194304 | tf_op jit(solution)/shard_map/all_to_all | solution.py:234
  308.9 1.3 copy-start.9
Sparse Core Ops, SparseCore 0:
  13.5 37.2 all-gather.4
  63.9 77.6 all-gather.8
  145.0 75.9 all-gather.6
  223.2 158.2 reduce-scatter.4
  383.6 146.7 reduce-scatter.2

commit v2 on v1

--- a/solution.py
+++ b/solution.py
@@ -13,7 +13,7 @@
 rope_base = 10000.0
 norm_eps = 1e-06
 masked_score = -1e30
-CHUNKS = 2
+CHUNK_ROWS = 2048
 
 
 def turn(block, cosine, sines):
@@ -127,17 +127,19 @@
     )(index, incoming)
 
 
-def expert_kernel(rows_ref, gate_ref, inner_ref, outer_ref, out_ref):
+def expert_kernel(rows_ref, gate_ref, pick_ref, inner_ref, outer_ref, out_ref):
+    gates = jnp.sum(gate_ref[...].astype(jnp.float32) * pick_ref[...], axis=1, keepdims=True)
     projected = jnp.dot(rows_ref[...], inner_ref[0], preferred_element_type=jnp.float32)
     half = projected.shape[1] // 2
     first = projected[:, :half]
     active = (first / (1.0 + jnp.exp(-first)) * projected[:, half:]).astype(jnp.bfloat16)
     out = jnp.dot(active, outer_ref[0], preferred_element_type=jnp.float32)
-    out_ref[...] = (out * gate_ref[...]).astype(jnp.bfloat16)
-
-
-def half_expert(rows, gates, inner, outer):
-    count, width = rows.shape
+    out_ref[...] = (out * gates).astype(jnp.bfloat16)
+
+
+def half_expert(rows, pick, inner, outer):
+    count, width = rows.shape[0], inner.shape[1]
+    extra = pick.shape[1]
     step = min(512, count)
     once = pl.Buffered(1)
     return pl.pallas_call(
@@ -145,7 +147,8 @@
         grid=(count // step,),
         in_specs=[
             pl.BlockSpec((step, width), lambda i: (i, 0)),
-            pl.BlockSpec((step, 1), lambda i: (i, 0)),
+            pl.BlockSpec((step, extra), lambda i: (i, width // extra)),
+            pl.BlockSpec((1, extra), lambda i: (0, 0)),
             pl.BlockSpec(inner.shape, lambda i: (0, 0, 0), pipeline_mode=once),
             pl.BlockSpec(outer.shape, lambda i: (0, 0, 0), pipeline_mode=once),
         ],
@@ -158,7 +161,18 @@
             transcendentals=0,
         ),
         name="half_expert",
-    )(rows, gates, inner, outer)
+    )(rows, rows, pick, inner, outer)
+
+
+def halve(blocks, member, distance):
+    groups, members, rows, width = blocks.shape
+    pairs = blocks.reshape(groups, members // 2, 2, rows, width)
+    bit = (member >> distance) % 2
+    kept = lax.dynamic_index_in_dim(pairs, bit, 2, keepdims=False)
+    handed = lax.dynamic_index_in_dim(pairs, 1 - bit, 2, keepdims=False)
+    swaps = [(i, i ^ 1 << distance) for i in range(lax.axis_size("exp"))]
+    received = lax.ppermute(handed, "exp", swaps)
+    return (kept.astype(jnp.float32) + received.astype(jnp.float32)).astype(jnp.bfloat16)
 
 
 def on_device(
@@ -213,13 +227,15 @@
 
     expert_range = jnp.arange(expert_count, dtype=jnp.int32)
     dense_gates = jnp.sum(
-        jnp.where(
-            expert_ids.T[None] == expert_range[:, None, None], gate_weights.T[None], 0.0
-        ),
+        jnp.where(expert_ids[:, :, None] == expert_range[None, None, :], gate_weights[:, :, None], 0.0),
         axis=1,
     )
-    all_gates = lax.all_gather(dense_gates, everyone, axis=0)
-    my_gates = lax.dynamic_index_in_dim(all_gates, expert, 1, keepdims=False)
+    high = dense_gates.astype(jnp.bfloat16)
+    low = (dense_gates - high.astype(jnp.float32)).astype(jnp.bfloat16)
+    spare = jnp.zeros((tok_rows, -2 * expert_count % 128), jnp.bfloat16)
+    gate_columns = jnp.concatenate([high, low, spare], axis=1)
+    lanes = jnp.arange(gate_columns.shape[1], dtype=jnp.int32)[None, :]
+    pick = ((lanes == expert) | (lanes == expert + expert_count)).astype(jnp.float32)
 
     group_range = jnp.arange(req_count, dtype=jnp.int32)
     page_range = jnp.arange(page_count, dtype=jnp.int32)
@@ -245,15 +261,21 @@
         hidden * lax.rsqrt(jnp.mean(hidden * hidden, axis=-1, keepdims=True) + norm_eps) * norm_gain
     ).astype(jnp.bfloat16)
 
-    part = tok_rows // CHUNKS
+    chunks = 2 if device_count * tok_rows <= 2 * CHUNK_ROWS else 4
+    part = tok_rows // chunks
+    payload = jnp.concatenate([normed, gate_columns], axis=1)
     sums = []
-    for chunk in range(CHUNKS):
+    for chunk in range(chunks):
         rows = slice(chunk * part, (chunk + 1) * part)
-        gathered = lax.all_gather(normed[rows], everyone, axis=0, tiled=True)
-        gates = my_gates[:, rows].reshape(-1, 1)
-        partial_out = half_expert(gathered, gates, expert_inner, expert_outer)
-        summed = lax.psum_scatter(partial_out, everyone, scatter_dimension=0, tiled=True)
-        sums.append(hidden[rows] + summed.astype(jnp.float32))
+        gathered = lax.all_gather(payload[rows], everyone, axis=0, tiled=True)
+        partial_out = half_expert(gathered, pick, expert_inner, expert_outer)
+        left = partial_out.reshape(req_count, member_count, part, model_width)
+        distance = 0
+        while left.shape[1] > 1:
+            left = halve(left, member, distance)
+            distance += 1
+        arrived = lax.all_to_all(left[:, 0], "req", split_axis=0, concat_axis=0, tiled=True)
+        sums.append(hidden[rows] + jnp.sum(arrived.astype(jnp.float32), axis=0))
     layer_out = jnp.concatenate(sums, axis=0).astype(jnp.bfloat16)
     return (layer_out, kv_pages)
 

time: 539 us -> 446 us (0.83)
  waiting for transfers between devices: 405 us -> 305 us
  blocking collectives: 41.9 us -> 0 us
  other arithmetic: 5.65 us -> 27.8 us
  starting transfers between devices: 4.38 us -> 18.1 us
  local copies, waits for them, and re-layouts: 13.7 us -> 24.8 us
    reduce_scatter x2 -> x0, waiting for transfers between devices: 216 us -> none  [on_device(): lax.psum_scatter(partial_out, everyone, scatter_dimension=0, tiled=True)]
    ppermute x0 -> x4, waiting for transfers between devices: none -> 91.8 us  [halve(): received = lax.ppermute(handed, 'exp', swaps)]
    all_to_all x1, waiting for transfers between devices: 57.2 us -> 0.01 us  [on_device(): lax.all_to_all(outgoing, 'req', split_axis=0, concat_axis=0, tiled=True)]
    all_gather x2, waiting for transfers between devices: 94.1 us -> 137 us  [on_device(): gathered = lax.all_gather(payload[rows], everyone, axis=0, tiled=True)]
    all_gather x1 -> x0, blocking collectives: 41.9 us -> none  [on_device(): all_gates = lax.all_gather(dense_gates, everyone, axis=0)]
    all_to_all x0 -> x2, waiting for transfers between devices: none -> 40.3 us  [on_device(): lax.all_to_all(left[:, 0], 'req', split_axis=0, concat_axis=0, tiled=True)]
    squeeze x0 -> x4, local copies, waits for them, and re-layouts: none -> 11.4 us  [halve(): handed = lax.dynamic_index_in_dim(pairs, 1 - bit, 2, keepdims=False)]
    all_to_all x0 -> x2, starting transfers between devices: none -> 11.1 us  [on_device(): lax.all_to_all(left[:, 0], 'req', split_axis=0, concat_axis=0, tiled=True)]
  transfers between devices with their start and end apart: 6 -> 10, of which waited for: 6 -> 6; matrix products, arithmetic and copies ran while one was open for 1% -> 8% of each run, Pallas kernels for 9% -> 11%
where the time goes in v2:
time: 446 us; the launch traced here: 445 us
  waiting for transfers between devices  305 us (68%)
  Pallas kernels  53.8 us (12%)
  other arithmetic  27.8 us (6%)
  local copies, waits for them, and re-layouts  24.8 us (6%)
  starting transfers between devices  18.1 us (4%)
  between operations  14 us (3%)
    all_gather x2, waiting for transfers between devices, on_device(): gathered = lax.all_gather(payload[rows], everyone, axis=0, tiled=True)  137 us
    ppermute x4, waiting for transfers between devices, halve(): received = lax.ppermute(handed, 'exp', swaps)  91.8 us
    all_to_all x2, waiting for transfers between devices, on_device(): lax.all_to_all(left[:, 0], 'req', split_axis=0, concat_axis=0, tiled=True)  40.3 us
    pallas_call x2, Pallas kernels, half_expert(): pl.pallas_call(expert_kernel, grid=(count // step,), in_specs=[pl.BlockSp...  36.4 us
    all_gather x1, waiting for transfers between devices, on_device(): keys_values = lax.all_gather(mine, 'exp', axis=0, tiled=True)  35.3 us
    squeeze x4, local copies, waits for them, and re-layouts, halve(): handed = lax.dynamic_index_in_dim(pairs, 1 - bit, 2, keepdims=False)  11.4 us
    all_to_all x2, starting transfers between devices, on_device(): lax.all_to_all(left[:, 0], 'req', split_axis=0, concat_axis=0, tiled=True)  11.1 us
    convert_element_type x2, other arithmetic, halve(): (kept.astype(jnp.float32) + received.astype(jnp.float32)).astype(jnp.bflo...  10.8 us
  transfers between devices with their start and end apart: 10, of which 6 were waited for; matrix products, arithmetic and copies ran while one was open for 8% of the time, Pallas kernels for 11%

profile of v2, /device:TPU:0, one launch (start us, length us, event | category | flops | bytes accessed | tf_op | source)
XLA Modules:
  0.0 445.1 jit_solution(16408645019210645921)
XLA Ops:
  7.2 0.0 copy-start.4
  7.2 0.0 all-gather.4.cloned.1.call-start
  7.3 0.8 dynamic_slice.21
  8.1 0.7 compare_convert_fusion
  8.7 0.8 multiply_reduce_fusion.2
  9.5 0.1 select_reduce_fusion.3
  9.6 0.3 fusion.6
  9.9 0.1 pad_maximum_fusion.1
  10.1 1.0 copy-done.1
  11.1 1.0 copy-done.2
  12.1 1.3 turn_keys.1
  13.4 0.0 all-gather.4.cloned.1.call-update
  13.4 0.0 all-gather.8.cloned.1.call-start
  13.5 0.7 select_reduce_fusion
  14.2 0.1 copy.24
  14.3 0.1 copy.25
  14.4 0.1 copy.26
  14.6 0.8 dynamic-slice_bitcast_fusion.2
  15.3 0.1 copy.23.mine_ref
  15.4 35.3 %all-gather.4.cloned.1.call-done.key_ref.value_ref = bf16[512,4096]{1,0:T(8,128)(2,1)} async-done(((bf16[128,4096]{1,0:T(8,128)(2,1)}), bf16[512,4096]{1,0:T(8,128)(2,1)}) %all-gather.4.cloned.1.call-update) | async-done | bytes 4194320 | tf_op jit(solution)/shard_map/all_gather | solution.py:226
  50.8 2.2 copy-done
  53.0 5.5 %attend.1 = bf16[128,2048]{1,0:T(8,128)(2,1)S(1)} custom-call(bf16[128,2048]{1,0:T(8,128)(2,1)S(1)} %copy-done.3, bf16[512,4096]{1,0:T(8,128)(2,1)S(1)} %copy-done, bf16[512,4096]{1,0:T(8,128)(2,1)S(1)} %copy-done, f32[128,128]{1,0:T(8,128)S(1)} %get-tuple-element.11.cos_ref, f32[128,128]{1,0:T(8,128)S(1)} %get-tuple-element.12.sin_ref, ...), custom_call_target="tpu_custom_call" | custom-call | tf_op jit(solution)/shard_map/attend/pallas_call | solution.py:67
  58.6 1.4 multiply_reduce_fusion
  60.0 0.9 multiply_convert_fusion
  61.0 1.8 concatenate.18
  62.8 1.9 fusion.7
  64.7 0.0 all-gather.8.cloned.1.call-update
  64.7 0.0 all-gather.6.cloned.1.call-start
  64.8 0.7 all-gather.6.cloned.1.call-update
  65.5 78.9 %all-gather.8.cloned.1.call-done.rows_ref.gate_ref = bf16[2048,2176]{1,0:T(8,128)(2,1)} async-done(((bf16[64,2176]{1,0:T(8,128)(2,1)}), bf16[2048,2176]{1,0:T(8,128)(2,1)}) %all-gather.8.cloned.1.call-update) | async-done | bytes 8912912 | tf_op jit(solution)/shard_map/all_gather | solution.py:270
  144.4 18.3 %half_expert.3 = bf16[2048,2048]{1,0:T(8,128)(2,1)} custom-call(bf16[2048,2176]{1,0:T(8,128)(2,1)} %all-gather.8.cloned.1.call-done.rows_ref.gate_ref, bf16[2048,2176]{1,0:T(8,128)(2,1)} %all-gather.8.cloned.1.call-done.rows_ref.gate_ref, f32[1,128]{1,0:T(1,128)S(1)} %or_convert_fusion.pick_ref, bf16[1,2048,1024]{2,1,0:T(8,128)(2,1)} %inner_ref.3, ...), custom_call_target="tpu_custom_call" | custom-call | flops 12884901888 | bytes 16777216 | tf_op jit(solution)/shard_map/half_expert/pallas_call | solution.py:145
  162.7 4.9 %dynamic-slice_bitcast_fusion = bf16[8,2,64,2048]{3,2,1,0:T(8,128)(2,1)} fusion(bf16[8,2,2,64,2048]{4,3,2,1,0:T(8,128)(2,1)} %bitcast.28, s32[]{:T(128)S(6)} %select_n.72), kind=kLoop, calls=%fused_computation.6 | loop fusion | bytes 8388612 | tf_op jit(solution)/shard_map/jit(dynamic_index_in_dim)/squeeze | solution.py:172
  167.6 0.3 collective-permute-start.2
  167.8 0.1 multiply_reduce_fusion.1
  167.9 58.1 %all-gather.6.cloned.1.call-done.rows_ref.gate_ref = bf16[2048,2176]{1,0:T(8,128)(2,1)} async-done(((bf16[64,2176]{1,0:T(8,128)(2,1)}), bf16[2048,2176]{1,0:T(8,128)(2,1)}) %all-gather.6.cloned.1.call-update) | async-done | bytes 8912912 | tf_op jit(solution)/shard_map/all_gather | solution.py:270
  226.0 18.2 %half_expert.2 = bf16[2048,2048]{1,0:T(8,128)(2,1)} custom-call(bf16[2048,2176]{1,0:T(8,128)(2,1)} %all-gather.6.cloned.1.call-done.rows_ref.gate_ref, bf16[2048,2176]{1,0:T(8,128)(2,1)} %all-gather.6.cloned.1.call-done.rows_ref.gate_ref, f32[1,128]{1,0:T(1,128)S(1)} %or_convert_fusion.pick_ref, bf16[1,2048,1024]{2,1,0:T(8,128)(2,1)} %inner_ref.3, ...), custom_call_target="tpu_custom_call" | custom-call | flops 12884901888 | bytes 16777216 | tf_op jit(solution)/shard_map/half_expert/pallas_call | solution.py:145
  244.2 4.8 %dynamic-slice_bitcast_fusion.1 = bf16[8,2,64,2048]{3,2,1,0:T(8,128)(2,1)} fusion(bf16[8,2,2,64,2048]{4,3,2,1,0:T(8,128)(2,1)} %bitcast.26, s32[]{:T(128)S(6)} %select_n.72), kind=kLoop, calls=%fused_computation.9 | loop fusion | bytes 8388612 | tf_op jit(solution)/shard_map/jit(dynamic_index_in_dim)/squeeze | solution.py:172
  249.0 0.3 collective-permute-start
  249.3 0.1 select_reduce_fusion.1
  249.3 0.6 pad_add_fusion.index_ref
  249.9 6.5 %pack_pages.1 = bf16[8,2,128,512]{3,2,1,0:T(8,128)(2,1)} custom-call(s32[9]{0:T(128)} %pad_add_fusion.index_ref, bf16[4,128,4096]{2,1,0:T(8,128)(2,1)} %bitcast.23, bf16[4,128,4096]{2,1,0:T(8,128)(2,1)} %bitcast.24), custom_call_target="tpu_custom_call" | custom-call | tf_op jit(solution)/shard_map/pack_pages/pallas_call | solution.py:93
  256.4 3.8 all-to-all-start.2
  260.2 5.4 %fusion = bf16[8,2,64,2048]{3,2,1,0:T(8,128)(2,1)S(1)} fusion(bf16[8,2,64,2048]{3,2,1,0:T(8,128)(2,1)} %collective-permute-done.2, bf16[8,2,2,64,2048]{4,3,2,1,0:T(8,128)(2,1)} %bitcast.29, s32[]{:T(128)S(6)} %select_n.71), kind=kLoop, calls=%fused_computation.1 | loop fusion | flops 8388608 | bytes 12582916 | tf_op jit(solution)/shard_map/convert_element_type | solution.py:175
  265.7 2.0 copy-done.7
  267.6 1.5 constant_dynamic-slice_fusion
  269.2 1.2 collective-permute-start.3
  270.4 46.8 %collective-permute-done.3 = bf16[8,1,64,2048]{3,2,1,0:T(8,128)(2,1)} collective-permute-done((bf16[8,1,64,2048]{3,2,1,0:T(8,128)(2,1)}, bf16[8,1,64,2048]{3,2,1,0:T(8,128)(2,1)}, u32[]{:S(2)}, u32[]{:S(2)}) %collective-permute-start.3) | collective-permute-done | bytes 2097184 | tf_op jit(solution)/shard_map/ppermute | solution.py:174
  317.3 4.5 %fusion.3 = bf16[8,64,2048]{2,1,0:T(8,128)(2,1)} fusion(bf16[8,1,64,2048]{3,2,1,0:T(8,128)(2,1)} %collective-permute-done.3, bf16[8,2,64,2048]{3,2,1,0:T(8,128)(2,1)} %copy-done.7, s32[]{:T(128)S(6)} %select_n.74), kind=kLoop, calls=%fused_computation.12 | loop fusion | flops 4194304 | bytes 6291460 | tf_op jit(solution)/shard_map/squeeze | solution.py:277
  321.8 1.4 copy-done.8
  323.1 5.4 %all-to-all-start.1 = ((bf16[8,64,2048]{2,1,0:T(8,128)(2,1)}), bf16[8,64,2048]{2,1,0:T(8,128)(2,1)S(1)}, u32[]{:S(2)}, u32[]{:S(2)}) async-start(bf16[8,64,2048]{2,1,0:T(8,128)(2,1)} %fusion.3), calls=%async_computation.1 | async-start | bytes 4194304 | tf_op jit(solution)/shard_map/all_to_all | solution.py:277
  328.6 5.4 %fusion.1 = bf16[8,2,64,2048]{3,2,1,0:T(8,128)(2,1)S(1)} fusion(bf16[8,2,64,2048]{3,2,1,0:T(8,128)(2,1)} %collective-permute-done, bf16[8,2,2,64,2048]{4,3,2,1,0:T(8,128)(2,1)} %bitcast.27, s32[]{:T(128)S(6)} %select_n.71), kind=kLoop, calls=%fused_computation.3 | loop fusion | flops 8388608 | bytes 12582916 | tf_op jit(solution)/shard_map/convert_element_type | solution.py:175
  334.0 0.2 constant_dynamic-slice_fusion.1
  334.2 1.3 collective-permute-start.1
  335.6 44.9 %collective-permute-done.1 = bf16[8,1,64,2048]{3,2,1,0:T(8,128)(2,1)S(1)} collective-permute-done((bf16[8,1,64,2048]{3,2,1,0:T(8,128)(2,1)S(1)}, bf16[8,1,64,2048]{3,2,1,0:T(8,128)(2,1)S(1)}, u32[]{:S(2)}, u32[]{:S(2)}) %collective-permute-start.1) | collective-permute-done | bytes 2097184 | tf_op jit(solution)/shard_map/ppermute | solution.py:174
  380.5 2.1 fusion.2
  382.6 5.7 %all-to-all-start = ((bf16[8,64,2048]{2,1,0:T(8,128)(2,1)}), bf16[8,64,2048]{2,1,0:T(8,128)(2,1)}, u32[]{:S(2)}, u32[]{:S(2)}) async-start(bf16[8,64,2048]{2,1,0:T(8,128)(2,1)} %fusion.2), calls=%async_computation | async-start | bytes 4194304 | tf_op jit(solution)/shard_map/all_to_all | solution.py:277
  388.4 0.1 compare_reduce_fusion
  388.5 0.6 select_reduce_fusion.2.index_ref
  389.1 4.0 place_pages.1
  393.1 1.1 convert_reduce_fusion
  394.3 40.3 %all-to-all-done = bf16[8,64,2048]{2,1,0:T(8,128)(2,1)} async-done(((bf16[8,64,2048]{2,1,0:T(8,128)(2,1)}), bf16[8,64,2048]{2,1,0:T(8,128)(2,1)}, u32[]{:S(2)}, u32[]{:S(2)}) %all-to-all-start) | async-done | bytes 2097184 | tf_op jit(solution)/shard_map/all_to_all | solution.py:277
  434.5 2.0 convert_reduce_fusion.1
  436.6 1.2 fusion.5
  437.7 0.8 pad_maximum_fusion
  (33 shorter events, 0.1 us)
Async XLA Ops:
  7.2 43.6 %copy-start.4 = (s32[512]{0:T(512)S(1)}, s32[512]{0:T(512)}, u32[]{:S(2)}) copy-start(s32[512]{0:T(512)} %param.18) | copy-start | bytes 6148
  7.2 43.6 %copy-start.3 = (bf16[128,2048]{1,0:T(8,128)(2,1)S(1)}, bf16[128,2048]{1,0:T(8,128)(2,1)}, u32[]{:S(2)}) copy-start(bf16[128,2048]{1,0:T(8,128)(2,1)} %query_ref.1) | copy-start | bytes 1572868
  7.2 43.6 %all-gather.4.cloned.1.call-start = ((), (), s32[]{:S(2)}) async-start(), calls=%async_computation.3 | async-start | bytes 5242880 | tf_op jit(solution)/shard_map/all_gather | solution.py:226
  10.0 1.0 copy-start.1
  11.1 1.0 copy-start.2
  13.4 131.0 %all-gather.8.cloned.1.call-start = ((), (), s32[]{:S(2)}) async-start(), calls=%async_computation.5 | async-start | bytes 9191424 | tf_op jit(solution)/shard_map/all_gather | solution.py:270
  50.8 2.2 copy-start
  53.0 5.6 %copy-start.6 = (bf16[2048,2048]{1,0:T(8,128)(2,1)S(1)}, bf16[2048,2048]{1,0:T(8,128)(2,1)}, u32[]{:S(2)}) copy-start(bf16[2048,2048]{1,0:T(8,128)(2,1)} %param.24) | copy-start | bytes 25165828
  53.0 5.6 %copy-start.9 = (bf16[128,2048]{1,0:T(8,128)(2,1)S(1)}, bf16[128,2048]{1,0:T(8,128)(2,1)}, u32[]{:S(2)}) copy-start(bf16[128,2048]{1,0:T(8,128)(2,1)} %param.14) | copy-start | bytes 1572868
  58.6 1.4 copy-start.10
  60.0 84.5 %copy-start.5 = (bf16[1,512,2048]{2,1,0:T(8,128)(2,1)S(1)}, bf16[1,512,2048]{2,1,0:T(8,128)(2,1)}, u32[]{:S(2)}) copy-start(bf16[1,512,2048]{2,1,0:T(8,128)(2,1)} %outer_ref.3) | copy-start | bytes 6291460
  64.7 161.3 %all-gather.6.cloned.1.call-start = ((), (), s32[]{:S(2)}) async-start(), calls=%async_computation.4 | async-start | bytes 9191424 | tf_op jit(solution)/shard_map/all_gather | solution.py:270
  162.7 5.1 %copy-start.11 = (s32[8,4]{0,1:T(4,128)S(1)}, s32[8,4]{0,1:T(4,128)}, u32[]{:S(2)}) copy-start(s32[8,4]{0,1:T(4,128)} %param.21) | copy-start | bytes 388
  167.6 92.7 %collective-permute-start.2 = (bf16[8,2,64,2048]{3,2,1,0:T(8,128)(2,1)}, bf16[8,2,64,2048]{3,2,1,0:T(8,128)(2,1)}, u32[]{:S(2)}, u32[]{:S(2)}) collective-permute-start(bf16[8,2,64,2048]{3,2,1,0:T(8,128)(2,1)} %dynamic-slice_bitcast_fusion), channel_id=1, source_target_pairs={{0,1},{1,0},{2,3},{3,2},{4,5},{5,4},{6,7},{7,6},{8,9},{9,8},{10,11... | collective-permute-start | bytes 12582920 | tf_op jit(solution)/shard_map/ppermute | solution.py:174
  249.0 79.6 %collective-permute-start = (bf16[8,2,64,2048]{3,2,1,0:T(8,128)(2,1)}, bf16[8,2,64,2048]{3,2,1,0:T(8,128)(2,1)}, u32[]{:S(2)}, u32[]{:S(2)}) collective-permute-start(bf16[8,2,64,2048]{3,2,1,0:T(8,128)(2,1)} %dynamic-slice_bitcast_fusion.1), channel_id=1, source_target_pairs={{0,1},{1,0},{2,3},{3,2},{4,5},{5,4},{6,7},{7,6},{8,9},{9,8},{10,11... | collective-permute-start | bytes 12582920 | tf_op jit(solution)/shard_map/ppermute | solution.py:174
  256.4 65.4 %all-to-all-start.2 = ((bf16[8,2,128,512]{3,2,1,0:T(8,128)(2,1)}), bf16[8,2,128,512]{3,2,1,0:T(8,128)(2,1)S(1)}, u32[]{:S(2)}, u32[]{:S(2)}) async-start(bf16[8,2,128,512]{3,2,1,0:T(8,128)(2,1)} %pack_pages.1), calls=%async_computation.2 | async-start | bytes 4194304 | tf_op jit(solution)/shard_map/all_to_all | solution.py:250
  265.6 2.0 copy-start.7
  269.2 48.1 %collective-permute-start.3 = (bf16[8,1,64,2048]{3,2,1,0:T(8,128)(2,1)}, bf16[8,1,64,2048]{3,2,1,0:T(8,128)(2,1)}, u32[]{:S(2)}, u32[]{:S(2)}) collective-permute-start(bf16[8,1,64,2048]{3,2,1,0:T(8,128)(2,1)} %constant_dynamic-slice_fusion), channel_id=1, source_target_pairs={{0,2},{1,3},{2,0},{3,1},{4,6},{5,7},{6,4},{7,5},{8,10},{9,11},{10,... | collective-permute-start | bytes 6291464 | tf_op jit(solution)/shard_map/ppermute | solution.py:174
  321.8 1.4 copy-start.8
  323.1 59.5 %all-to-all-start.1 = ((bf16[8,64,2048]{2,1,0:T(8,128)(2,1)}), bf16[8,64,2048]{2,1,0:T(8,128)(2,1)S(1)}, u32[]{:S(2)}, u32[]{:S(2)}) async-start(bf16[8,64,2048]{2,1,0:T(8,128)(2,1)} %fusion.3), calls=%async_computation.1 | async-start | bytes 4194304 | tf_op jit(solution)/shard_map/all_to_all | solution.py:277
  334.2 54.2 %copy-start.12 = (s32[8]{0:T(128)S(1)}, s32[8]{0:T(128)}, u32[]{:S(2)}) copy-start(s32[8]{0:T(128)} %param.20) | copy-start | bytes 100
  334.2 46.3 %collective-permute-start.1 = (bf16[8,1,64,2048]{3,2,1,0:T(8,128)(2,1)S(1)}, bf16[8,1,64,2048]{3,2,1,0:T(8,128)(2,1)S(1)}, u32[]{:S(2)}, u32[]{:S(2)}) collective-permute-start(bf16[8,1,64,2048]{3,2,1,0:T(8,128)(2,1)S(1)} %constant_dynamic-slice_fusion.1), channel_id=1, source_target_pairs={{0,2},{1,3},{2,0},{3,1},{4,6},{5,7},{6,4},{7,5},{8,10},{9,11},{10,... | collective-permute-start | bytes 6291464 | tf_op jit(solution)/shard_map/ppermute | solution.py:174
  382.6 51.9 %all-to-all-start = ((bf16[8,64,2048]{2,1,0:T(8,128)(2,1)}), bf16[8,64,2048]{2,1,0:T(8,128)(2,1)}, u32[]{:S(2)}, u32[]{:S(2)}) async-start(bf16[8,64,2048]{2,1,0:T(8,128)(2,1)} %fusion.2), calls=%async_computation | async-start | bytes 4194304 | tf_op jit(solution)/shard_map/all_to_all | solution.py:277
Sparse Core Ops, SparseCore 0:
  13.6 37.1 all-gather.3
  64.8 79.5 all-gather.7
  147.8 78.1 all-gather.5
